TPU v7x, 32 devices: a whole 2x2x4 slice. The times are simulated.
32 devices in a mesh: groups: 2 (over y), chan: 4 (over z), space: 2 (over x), dp: 2 (over core).
Axes of the slice: x: 2, y: 2, z: 4, core: 2. Of those that a mesh axis runs over, the one named last changes fastest.
Arguments:
- inputs: bfloat16 [4, 4, 16, 16, 512], P(('groups', 'dp'), 'space', None, None, 'chan'), parts along dimension 0, may hold values from -6 to 6
- weights: bfloat16 [27, 512, 512], P(None, 'chan'), may hold values from -0.0625 to 0.0625
- bias: float32 [512], P('chan'), may hold values from -3 to 3
- upstream: bfloat16 [4, 4, 16, 16, 512], P(('groups', 'dp'), 'space', None, None, 'chan'), parts along dimension 0, may hold values from -6 to 6
Outputs:
- activated: bfloat16 [4, 4, 16, 16, 512], P(('groups', 'dp'), 'space', None, None, 'chan'), parts along dimension 0
- grad_inputs: bfloat16 [4, 4, 16, 16, 512], P(('groups', 'dp'), 'space', None, None, 'chan'), parts along dimension 0
- grad_weights: float32 [54, 512, 512], P('groups', 'chan', ('space', 'dp')), parts along dimension 0
There are 2 independent parts, one for each index of `groups`. A program takes and returns all parts, laid end to end along the dimension named above; an argument that names none is the same for every part. Nothing has to cross between parts.
All inputs are finite; a program needn't handle non-finite values.
Results may differ from a plain program's by a relative error of at most 0.0049.
Values may be sent and summed in bfloat16 or wider, within the bound.
A program may use at most 64 MiB of HBM per device.

v0:
```python
import math
import jax
import jax.numpy as jnp
from jax import lax
from jax.sharding import PartitionSpec as P

tap_offsets = [(a, b, c) for a in (-1, 0, 1) for b in (-1, 0, 1) for c in (-1, 0, 1)]


def extended(array, sides, width):
    for axis, dim in sides:
        size, length = (lax.axis_size(axis), array.shape[dim])
        up = [(i, (i + 1) % size) for i in range(size - 1)]
        down = [(j, i) for i, j in up]
        last = lax.slice_in_dim(array, length - width, length, axis=dim)
        leading = lax.slice_in_dim(array, 0, width, axis=dim)
        before = lax.ppermute(last, axis, up)
        after = lax.ppermute(leading, axis, down)
        array = jnp.concatenate([before, array, after], axis=dim)
    return array


def spatial_pad(volume):
    return jnp.pad(volume, ((0, 0), (0, 0), (1, 1), (1, 1), (0, 0)))


def tap_slice(volume, a, b, c, width_x, width_y, width_z):
    return volume[:, 1 + a : 1 + a + width_x, 1 + b : 1 + b + width_y, 1 + c : 1 + c + width_z]


def local(inputs, weights, bias, upstream):
    batch_size, width_x, width_y, width_z, group_width = inputs.shape
    voxels = batch_size * width_x * width_y * width_z
    tap_count = weights.shape[0]
    outputs_all = weights.shape[2]
    bordered = spatial_pad(extended(inputs, (("space", 1),), 1))
    stacked = jnp.concatenate(
        [
            tap_slice(bordered, a, b, c, width_x, width_y, width_z).reshape(voxels, group_width)
            for a, b, c in tap_offsets
        ],
        axis=1,
    )
    flat_weights = weights.reshape(tap_count * group_width, outputs_all)
    out_share = outputs_all // lax.axis_size("chan")
    summed = lax.psum_scatter(
        lax.dot_general(
            flat_weights, stacked, (((0,), (1,)), ((), ())), preferred_element_type=jnp.float32
        ),
        "chan",
        scatter_dimension=0,
        tiled=True,
    ).T
    preact = summed + bias[None, :]
    gate_value = jax.nn.sigmoid(preact)
    activated = (
        (preact * gate_value)
        .astype(jnp.bfloat16)
        .reshape(batch_size, width_x, width_y, width_z, out_share)
    )
    grad_flat = (
        upstream.reshape(voxels, out_share).astype(jnp.float32)
        * gate_value
        * (1.0 + preact * (1.0 - gate_value))
    )
    grad_pre = grad_flat.astype(jnp.bfloat16).reshape(
        batch_size, width_x, width_y, width_z, out_share
    )
    grad_full = lax.all_gather(grad_pre, "chan", axis=4, tiled=True)
    framed = extended(grad_full, (("space", 1),), 1)
    interior = framed[:, 1:-1].reshape(voxels, outputs_all)
    framed_all = spatial_pad(framed)
    padded_shape = framed_all.shape
    projected = lax.dot_general(
        framed_all.reshape(-1, outputs_all),
        flat_weights,
        (((1,), (1,)), ((), ())),
        preferred_element_type=jnp.float32,
    )
    projected = projected.reshape(
        padded_shape[0], padded_shape[1], padded_shape[2], padded_shape[3], tap_count, group_width
    )
    grad_in = jnp.zeros((batch_size, width_x, width_y, width_z, group_width), jnp.float32)
    for k, (a, b, c) in enumerate(tap_offsets):
        grad_in = (
            grad_in
            + projected[
                :, 1 - a : 1 - a + width_x, 1 - b : 1 - b + width_y, 1 - c : 1 - c + width_z, k, :
            ]
        )
    grad_inputs = grad_in.astype(jnp.bfloat16)
    weight_partial = lax.dot_general(
        stacked, interior, (((0,), (0,)), ((), ())), preferred_element_type=jnp.float32
    )
    weight_partial = weight_partial.reshape(tap_count, group_width, outputs_all)
    reduced = lax.psum_scatter(weight_partial, ("space", "dp"), scatter_dimension=2, tiled=True)
    total_voxels = voxels * lax.axis_size("space") * lax.axis_size("dp")
    grad_weights = reduced * (1.0 / math.sqrt(total_voxels))
    return (activated, grad_inputs, grad_weights)


def solution(mesh):
    return jax.shard_map(
        local,
        mesh=mesh,
        in_specs=(
            P(("groups", "dp"), "space", None, None, "chan"),
            P(None, "chan", None),
            P("chan"),
            P(("groups", "dp"), "space", None, None, "chan"),
        ),
        out_specs=(
            P(("groups", "dp"), "space", None, None, "chan"),
            P(("groups", "dp"), "space", None, None, "chan"),
            P("groups", "chan", ("space", "dp")),
        ),
        check_vma=False,
    )
```

profile of v0, /device:TPU:0, one launch (start us, length us, event | category | flops | bytes accessed | tf_op | source)
XLA Modules:
  0.0 212.0 jit_solution(125363186464683135)
XLA Ops:
  7.2 1.7 fusion.69
  8.9 5.5 %collective-permute-start = (bf16[1,1,16,16,128]{4,3,2,1,0:T(8,128)(2,1)}, bf16[1,1,16,16,128]{4,3,2,1,0:T(8,128)(2,1)}, u32[]{:S(2)}, u32[]{:S(2)}) collective-permute-start(bf16[1,1,16,16,128]{4,3,2,1,0:T(8,128)(2,1)} %get-tuple-element.33), channel_id=1, source_target_pairs={{0,2},{1,3},{4,6},{5,7},{8,10},{9,11},{12,14},{13,15},{16,18},{17,... | collective-permute-start | bytes 196616 | tf_op jit(solution)/shard_map/ppermute | solution.py:17
  14.4 1.3 collective-permute-start.1
  15.6 1.7 copy.20
  17.3 3.5 %collective-permute-done.1 = bf16[1,1,16,16,128]{4,3,2,1,0:T(8,128)(2,1)} collective-permute-done((bf16[1,1,16,16,128]{4,3,2,1,0:T(8,128)(2,1)}, bf16[1,1,16,16,128]{4,3,2,1,0:T(8,128)(2,1)}, u32[]{:S(2)}, u32[]{:S(2)}) %collective-permute-start.1) | collective-permute-done | bytes 65568 | tf_op jit(solution)/shard_map/ppermute | solution.py:18
  20.8 1.1 select_maximum_fusion.3
  22.8 1.5 fusion.67
  24.3 1.6 pad_maximum_fusion
  26.0 1.7 copy.29
  27.6 1.7 copy.11
  29.3 1.7 copy.12
  30.9 1.7 copy.10
  32.6 1.7 copy.9
  34.3 1.7 copy.8
  35.9 1.7 copy.7
  37.6 1.7 copy.33
  39.2 1.7 copy.32
  40.9 1.7 copy.31
  42.6 1.7 copy.30
  44.2 1.7 copy.28
  45.9 1.7 copy.27
  47.6 1.7 copy.26
  49.2 1.7 copy.25
  50.9 1.7 copy.24
  52.5 1.7 copy.23
  54.2 1.7 copy.22
  55.9 1.7 copy.21
  57.5 1.7 copy.19
  59.2 1.7 copy.18
  60.9 1.7 copy.17
  62.5 1.7 copy.16
  64.2 1.7 copy.15
  65.8 1.7 copy.14
  67.5 1.7 copy.13
  82.6 1.9 copy-done.2
  84.5 3.0 %convolution_bitcast_fusion.1 = f32[512,512]{0,1:T(8,128)} fusion(bf16[512,3456]{0,1:T(8,128)(2,1)S(1)} %constant_dynamic-update-slice_fusion, bf16[3456,512]{1,0:T(8,128)(2,1)S(1)} %bitcast.262), kind=kOutput, calls=%fused_computation.21 | convolution fusion | flops 1811939328 | bytes 8126464 | tf_op jit(solution)/shard_map/dot_general | solution.py:47
  87.6 27.6 %reduce-scatter.3.cloned.1.call-done = f32[128,512]{0,1:T(8,128)} async-done(((f32[512,512]{0,1:T(8,128)}), f32[128,512]{0,1:T(8,128)}) %reduce-scatter.3.cloned.1.call-update) | async-done | bytes 262160 | tf_op jit(solution)/shard_map/reduce_scatter | solution.py:46
  115.2 1.8 fusion.56
  117.0 15.3 %all_gather.3 = bf16[1,2,16,16,512]{4,3,2,1,0:T(8,128)(2,1)S(1)} all-gather(bf16[1,2,16,16,128]{4,3,2,1,0:T(8,128)(2,1)S(1)} %bitcast.290), channel_id=1, replica_groups=mesh['groups'=2,'chan'=4,'space'=2,'dp'=2] {'chan'}, dimensions={4}, use_global_device_ids=true | all-gather | bytes 655360 | tf_op jit(solution)/shard_map/all_gather | solution.py:69
  133.1 6.9 %fusion.70 = f32[27,128,512]{2,1,0:T(8,128)} fusion(bf16[27,128,512]{2,1,0:T(8,128)(2,1)} %bitcast.264, bf16[512,512,1]{1,0,2:T(8,128)(2,1)S(1)} %bitcast.263), kind=kOutput, calls=%fused_computation.139 | convolution fusion | flops 1811939328 | bytes 11141120 | tf_op jit(solution)/shard_map/dot_general | solution.py:92
  141.1 3.3 %collective-permute-start.2 = (bf16[1,1,16,16,512]{4,3,2,1,0:T(8,128)(2,1)S(1)}, bf16[1,1,16,16,512]{4,3,2,1,0:T(8,128)(2,1)S(1)}, u32[]{:S(2)}, u32[]{:S(2)}) collective-permute-start(bf16[1,1,16,16,512]{4,3,2,1,0:T(8,128)(2,1)S(1)} %get-tuple-element.3), channel_id=1, source_target_pairs={{0,2},{1,3},{4,6},{5,7},{8,10},{9,11},{12,14},{13,15},{16,18},{17,... | collective-permute-start | bytes 786440 | tf_op jit(solution)/shard_map/ppermute | solution.py:17
  144.4 1.3 collective-permute-start.3
  145.7 2.6 %collective-permute-done.2 = bf16[1,1,16,16,512]{4,3,2,1,0:T(8,128)(2,1)S(1)} collective-permute-done((bf16[1,1,16,16,512]{4,3,2,1,0:T(8,128)(2,1)S(1)}, bf16[1,1,16,16,512]{4,3,2,1,0:T(8,128)(2,1)S(1)}, u32[]{:S(2)}, u32[]{:S(2)}) %collective-permute-start.2) | collective-permute-done | bytes 262176 | tf_op jit(solution)/shard_map/ppermute | solution.py:17
  148.2 4.4 %collective-permute-done.3 = bf16[1,1,16,16,512]{4,3,2,1,0:T(8,128)(2,1)S(1)} collective-permute-done((bf16[1,1,16,16,512]{4,3,2,1,0:T(8,128)(2,1)S(1)}, bf16[1,1,16,16,512]{4,3,2,1,0:T(8,128)(2,1)S(1)}, u32[]{:S(2)}, u32[]{:S(2)}) %collective-permute-start.3) | collective-permute-done | bytes 262176 | tf_op jit(solution)/shard_map/ppermute | solution.py:18
  152.6 8.2 %convolution_bitcast_fusion = f32[1,4,18,18,27,128]{5,3,4,2,1,0:T(8,128)S(1)} fusion(bf16[27,128,512]{2,1,0:T(8,128)(2,1)S(1)} %copy-done, bf16[1,1,16,16,512]{4,3,2,1,0:T(8,128)(2,1)S(1)} %collective-permute-done.3, bf16[1,2,16,16,512]{4,3,2,1,0:T(8,128)(2,1)} %copy-done.1, bf16[1,1,16,16,512]{4,3,2,1,0:T(8,128)(2,1)S(1)} %collective-permute-done.2), kind=kOutput, calls=%fused_computation | convolution fusion | flops 4599078912 | bytes 22503424 | tf_op jit(solution)/shard_map/dot_general | solution.py:74
  160.8 1.2 fusion.28
  162.0 40.2 %reduce-scatter.5.cloned.1.call-done = f32[27,128,128]{2,1,0:T(8,128)} async-done(((f32[27,128,512]{2,1,0:T(8,128)}), f32[27,128,128]{2,1,0:T(8,128)}) %reduce-scatter.5.cloned.1.call-update) | async-done | bytes 1769488 | tf_op jit(solution)/shard_map/reduce_scatter | solution.py:96
  202.2 2.9 %broadcast_multiply_fusion = f32[27,128,128]{2,1,0:T(8,128)} fusion(f32[27,128,128]{2,1,0:T(8,128)} %reduce-scatter.5.cloned.1.call-done), kind=kLoop, calls=%fused_computation.27 | loop fusion | flops 442368 | bytes 3538944 | tf_op jit(solution)/shard_map/mul | solution.py:98
  (69 shorter events, 16.0 us)
Async XLA Ops:
  7.2 75.5 %copy-start = (bf16[27,128,512]{2,1,0:T(8,128)(2,1)S(1)}, bf16[27,128,512]{2,1,0:T(8,128)(2,1)}, u32[]{:S(2)}) copy-start(bf16[27,128,512]{2,1,0:T(8,128)(2,1)} %param.5) | copy-start | bytes 10616836
  7.2 108.0 %reduce-scatter.3.cloned.1.call-start = ((), (), s32[]{:S(2)}) async-start(), calls=%async_computation.2 | async-start | bytes 1310720 | tf_op jit(solution)/shard_map/reduce_scatter | solution.py:46
  8.9 8.4 %collective-permute-start = (bf16[1,1,16,16,128]{4,3,2,1,0:T(8,128)(2,1)}, bf16[1,1,16,16,128]{4,3,2,1,0:T(8,128)(2,1)}, u32[]{:S(2)}, u32[]{:S(2)}) collective-permute-start(bf16[1,1,16,16,128]{4,3,2,1,0:T(8,128)(2,1)} %get-tuple-element.33), channel_id=1, source_target_pairs={{0,2},{1,3},{4,6},{5,7},{8,10},{9,11},{12,14},{13,15},{16,18},{17,... | collective-permute-start | bytes 196616 | tf_op jit(solution)/shard_map/ppermute | solution.py:17
  14.4 6.5 %collective-permute-start.1 = (bf16[1,1,16,16,128]{4,3,2,1,0:T(8,128)(2,1)}, bf16[1,1,16,16,128]{4,3,2,1,0:T(8,128)(2,1)}, u32[]{:S(2)}, u32[]{:S(2)}) collective-permute-start(bf16[1,1,16,16,128]{4,3,2,1,0:T(8,128)(2,1)} %get-tuple-element.34), channel_id=1, source_target_pairs={{2,0},{3,1},{6,4},{7,5},{10,8},{11,9},{14,12},{15,13},{18,16},{19,... | collective-permute-start | bytes 196616 | tf_op jit(solution)/shard_map/ppermute | solution.py:18
  17.3 7.0 %copy-start.3 = (bf16[1,2,16,16,128]{4,3,2,1,0:T(8,128)(2,1)S(1)}, bf16[1,2,16,16,128]{4,3,2,1,0:T(8,128)(2,1)}, u32[]{:S(2)}) copy-start(bf16[1,2,16,16,128]{4,3,2,1,0:T(8,128)(2,1)} %param.4) | copy-start | bytes 393220
  69.2 13.1 %copy-start.16 = (bf16[512,128]{0,1:T(8,128)(2,1)S(1)}, bf16[512,128]{0,1:T(8,128)(2,1)}, u32[]{:S(2)}) copy-start(bf16[512,128]{0,1:T(8,128)(2,1)} %copy.21) | copy-start | bytes 393220
  69.2 13.1 %copy-start.15 = (bf16[512,128]{0,1:T(8,128)(2,1)S(1)}, bf16[512,128]{0,1:T(8,128)(2,1)}, u32[]{:S(2)}) copy-start(bf16[512,128]{0,1:T(8,128)(2,1)} %copy.22) | copy-start | bytes 393220
  69.2 13.2 %copy-start.14 = (bf16[512,128]{0,1:T(8,128)(2,1)S(1)}, bf16[512,128]{0,1:T(8,128)(2,1)}, u32[]{:S(2)}) copy-start(bf16[512,128]{0,1:T(8,128)(2,1)} %copy.23) | copy-start | bytes 393220
  69.2 13.2 %copy-start.13 = (bf16[512,128]{0,1:T(8,128)(2,1)S(1)}, bf16[512,128]{0,1:T(8,128)(2,1)}, u32[]{:S(2)}) copy-start(bf16[512,128]{0,1:T(8,128)(2,1)} %copy.24) | copy-start | bytes 393220
  69.2 13.2 %copy-start.12 = (bf16[512,128]{0,1:T(8,128)(2,1)S(1)}, bf16[512,128]{0,1:T(8,128)(2,1)}, u32[]{:S(2)}) copy-start(bf16[512,128]{0,1:T(8,128)(2,1)} %copy.25) | copy-start | bytes 393220
  69.2 13.2 %copy-start.11 = (bf16[512,128]{0,1:T(8,128)(2,1)S(1)}, bf16[512,128]{0,1:T(8,128)(2,1)}, u32[]{:S(2)}) copy-start(bf16[512,128]{0,1:T(8,128)(2,1)} %copy.26) | copy-start | bytes 393220
  69.2 13.2 %copy-start.10 = (bf16[512,128]{0,1:T(8,128)(2,1)S(1)}, bf16[512,128]{0,1:T(8,128)(2,1)}, u32[]{:S(2)}) copy-start(bf16[512,128]{0,1:T(8,128)(2,1)} %copy.27) | copy-start | bytes 393220
  69.2 13.3 %copy-start.9 = (bf16[512,128]{0,1:T(8,128)(2,1)S(1)}, bf16[512,128]{0,1:T(8,128)(2,1)}, u32[]{:S(2)}) copy-start(bf16[512,128]{0,1:T(8,128)(2,1)} %copy.28) | copy-start | bytes 393220
  69.2 13.3 %copy-start.4 = (bf16[512,128]{0,1:T(8,128)(2,1)S(1)}, bf16[512,128]{0,1:T(8,128)(2,1)}, u32[]{:S(2)}) copy-start(bf16[512,128]{0,1:T(8,128)(2,1)} %copy.29) | copy-start | bytes 393220
  69.2 13.3 %copy-start.8 = (bf16[512,128]{0,1:T(8,128)(2,1)S(1)}, bf16[512,128]{0,1:T(8,128)(2,1)}, u32[]{:S(2)}) copy-start(bf16[512,128]{0,1:T(8,128)(2,1)} %copy.30) | copy-start | bytes 393220
  69.2 13.3 %copy-start.7 = (bf16[512,128]{0,1:T(8,128)(2,1)S(1)}, bf16[512,128]{0,1:T(8,128)(2,1)}, u32[]{:S(2)}) copy-start(bf16[512,128]{0,1:T(8,128)(2,1)} %copy.31) | copy-start | bytes 393220
  69.2 13.3 %copy-start.6 = (bf16[512,128]{0,1:T(8,128)(2,1)S(1)}, bf16[512,128]{0,1:T(8,128)(2,1)}, u32[]{:S(2)}) copy-start(bf16[512,128]{0,1:T(8,128)(2,1)} %copy.32) | copy-start | bytes 393220
  69.2 13.4 %copy-start.5 = (bf16[512,128]{0,1:T(8,128)(2,1)S(1)}, bf16[512,128]{0,1:T(8,128)(2,1)}, u32[]{:S(2)}) copy-start(bf16[512,128]{0,1:T(8,128)(2,1)} %copy.33) | copy-start | bytes 393220
  82.6 1.9 copy-start.2
  84.5 30.7 %copy-start.17 = (f32[128]{0:T(128)S(1)}, f32[128]{0:T(128)}, u32[]{:S(2)}) copy-start(f32[128]{0:T(128)} %param.6) | copy-start | bytes 1540
  87.6 114.6 %reduce-scatter.5.cloned.1.call-start = ((), (), s32[]{:S(2)}) async-start(), calls=%async_computation.3 | async-start | bytes 8847360 | tf_op jit(solution)/shard_map/reduce_scatter | solution.py:96
  132.3 0.8 copy-start.1
  141.1 7.1 %collective-permute-start.2 = (bf16[1,1,16,16,512]{4,3,2,1,0:T(8,128)(2,1)S(1)}, bf16[1,1,16,16,512]{4,3,2,1,0:T(8,128)(2,1)S(1)}, u32[]{:S(2)}, u32[]{:S(2)}) collective-permute-start(bf16[1,1,16,16,512]{4,3,2,1,0:T(8,128)(2,1)S(1)} %get-tuple-element.3), channel_id=1, source_target_pairs={{0,2},{1,3},{4,6},{5,7},{8,10},{9,11},{12,14},{13,15},{16,18},{17,... | collective-permute-start | bytes 786440 | tf_op jit(solution)/shard_map/ppermute | solution.py:17
  144.4 8.3 %collective-permute-start.3 = (bf16[1,1,16,16,512]{4,3,2,1,0:T(8,128)(2,1)S(1)}, bf16[1,1,16,16,512]{4,3,2,1,0:T(8,128)(2,1)S(1)}, u32[]{:S(2)}, u32[]{:S(2)}) collective-permute-start(bf16[1,1,16,16,512]{4,3,2,1,0:T(8,128)(2,1)S(1)} %get-tuple-element.4), channel_id=1, source_target_pairs={{2,0},{3,1},{6,4},{7,5},{10,8},{11,9},{14,12},{15,13},{18,16},{19,... | collective-permute-start | bytes 786440 | tf_op jit(solution)/shard_map/ppermute | solution.py:18
Sparse Core Ops, SparseCore 0:
  87.7 27.4 reduce-scatter.2
  140.1 62.0 reduce-scatter.4
where the time goes:
time: 213 us; the launch traced here: 212 us
  waiting for transfers between devices  78.3 us (37%)
  local copies, waits for them, and re-layouts  65.8 us (31%)
  matrix products  18.1 us (8%)
  blocking collectives  15.3 us (7%)
  between operations  14.5 us (7%)
  starting transfers between devices  11.4 us (5%)
  other arithmetic  8.62 us (4%)
    reshape x27, local copies, waits for them, and re-layouts, local(): tap_slice(bordered, a, b, c, width_x, width_y, width_z)  44.9 us
    reduce_scatter x1, waiting for transfers between devices, local(): lax.psum_scatter(weight_partial, ('space', 'dp'), scatter_dimension=2, ti...  40.2 us
    reduce_scatter x1, waiting for transfers between devices, local(): lax.psum_scatter(lax.dot_general(flat_weights, stacked, (((0,), (1,)), ((...  27.6 us
    unnamed x62, local copies, waits for them, and re-layouts  15.8 us
    all_gather x1, blocking collectives, local(): grad_full = lax.all_gather(grad_pre, 'chan', axis=4, tiled=True)  15.3 us
    ppermute x2, starting transfers between devices, extended(): before = lax.ppermute(last, axis, up)  8.73 us
    dot_general x1, matrix products, local(): lax.dot_general(framed_all.reshape(-1, outputs_all), flat_weights, (((1,)...  8.15 us
    ppermute x2, waiting for transfers between devices, extended(): after = lax.ppermute(leading, axis, down)  7.9 us
  transfers between devices with their start and end apart: 6, of which 5 were waited for; matrix products, arithmetic and copies ran while one was open for 6% of the time, Pallas kernels for 0%

commit v1 on v0

--- a/solution.py
+++ b/solution.py
@@ -66,7 +66,16 @@
     grad_pre = grad_flat.astype(jnp.bfloat16).reshape(
         batch_size, width_x, width_y, width_z, out_share
     )
-    grad_full = lax.all_gather(grad_pre, "chan", axis=4, tiled=True)
+    x_now, left_arr = (lax.psum(1, axis_name="chan"), lax.axis_index("chan"))
+    grad_full, part_next = (grad_pre, 1)
+    while part_next < x_now:
+        z1 = lax.ppermute(
+            grad_full, axis_name="chan", perm=[(jj, jj ^ part_next) for jj in range(x_now)]
+        )
+        v_now = jnp.concatenate([grad_full, z1], axis=4)
+        y1 = jnp.concatenate([z1, grad_full], axis=4)
+        grad_full = jnp.where(left_arr & part_next == 0, v_now, y1)
+        part_next = 2 * part_next
     framed = extended(grad_full, (("space", 1),), 1)
     interior = framed[:, 1:-1].reshape(voxels, outputs_all)
     framed_all = spatial_pad(framed)

time: 213 us -> 218 us (1.023)
  waiting for transfers between devices: 78.3 us -> 94.7 us
  blocking collectives: 15.3 us -> 0 us
  other arithmetic: 8.62 us -> 14 us
    ppermute x0 -> x2, waiting for transfers between devices: none -> 16.8 us  [local(): lax.ppermute(grad_full, axis_name='chan', perm=[(jj, jj ^ part_next) for...]
    all_gather x1 -> x0, blocking collectives: 15.3 us -> none  [local(): grad_full = lax.all_gather(grad_pre, 'chan', axis=4, tiled=True)]
    select_n x0 -> x3, other arithmetic: none -> 4.2 us  [local(): grad_full = jnp.where(left_arr & part_next == 0, v_now, y1)]
    unnamed x62 -> x60, local copies, waits for them, and re-layouts: 15.8 us -> 15 us
  transfers between devices with their start and end apart: 6 -> 8, of which waited for: 5 -> 7; matrix products, arithmetic and copies ran while one was open for 6% -> 6% of each run, Pallas kernels for 0% -> 0%
where the time goes in v1:
time: 218 us; the launch traced here: 217 us
  waiting for transfers between devices  94.7 us (43%)
  local copies, waits for them, and re-layouts  63.9 us (29%)
  matrix products  16.7 us (8%)
  between operations  14.5 us (7%)
  other arithmetic  14 us (6%)
  starting transfers between devices  12.9 us (6%)
    reshape x27, local copies, waits for them, and re-layouts, local(): tap_slice(bordered, a, b, c, width_x, width_y, width_z)  44.7 us
    reduce_scatter x1, waiting for transfers between devices, local(): lax.psum_scatter(weight_partial, ('space', 'dp'), scatter_dimension=2, ti...  38.5 us
    reduce_scatter x1, waiting for transfers between devices, local(): lax.psum_scatter(lax.dot_general(flat_weights, stacked, (((0,), (1,)), ((...  27.6 us
    ppermute x2, waiting for transfers between devices, local(): lax.ppermute(grad_full, axis_name='chan', perm=[(jj, jj ^ part_next) for...  16.8 us
    unnamed x60, local copies, waits for them, and re-layouts  15 us
    ppermute x2, starting transfers between devices, extended(): before = lax.ppermute(last, axis, up)  8.84 us
    ppermute x2, waiting for transfers between devices, extended(): after = lax.ppermute(leading, axis, down)  7.64 us
    dot_general x1, matrix products, local(): lax.dot_general(stacked, interior, (((0,), (0,)), ((), ())), preferred_el...  6.97 us
  transfers between devices with their start and end apart: 8, of which 7 were waited for; matrix products, arithmetic and copies ran while one was open for 6% of the time, Pallas kernels for 0%

profile of v1, /device:TPU:0, one launch (start us, length us, event | category | flops | bytes accessed | tf_op | source)
XLA Modules:
  0.0 216.8 jit_solution(15230322517483690376)
XLA Ops:
  7.2 1.7 fusion.80
  8.9 5.5 %collective-permute-start = (bf16[1,1,16,16,128]{4,3,2,1,0:T(8,128)(2,1)}, bf16[1,1,16,16,128]{4,3,2,1,0:T(8,128)(2,1)}, u32[]{:S(2)}, u32[]{:S(2)}) collective-permute-start(bf16[1,1,16,16,128]{4,3,2,1,0:T(8,128)(2,1)} %get-tuple-element.33), channel_id=1, source_target_pairs={{0,2},{1,3},{4,6},{5,7},{8,10},{9,11},{12,14},{13,15},{16,18},{17,... | collective-permute-start | bytes 196616 | tf_op jit(solution)/shard_map/ppermute | solution.py:17
  14.4 1.3 collective-permute-start.1
  15.7 1.7 copy.20
  17.3 3.5 %collective-permute-done.1 = bf16[1,1,16,16,128]{4,3,2,1,0:T(8,128)(2,1)} collective-permute-done((bf16[1,1,16,16,128]{4,3,2,1,0:T(8,128)(2,1)}, bf16[1,1,16,16,128]{4,3,2,1,0:T(8,128)(2,1)}, u32[]{:S(2)}, u32[]{:S(2)}) %collective-permute-start.1) | collective-permute-done | bytes 65568 | tf_op jit(solution)/shard_map/ppermute | solution.py:18
  22.8 1.5 fusion.78
  24.4 1.6 pad_maximum_fusion
  26.0 1.7 copy.29
  27.6 1.7 copy.11
  29.3 1.7 copy.12
  30.9 1.7 copy.10
  32.6 1.6 copy.9
  34.2 1.7 copy.8
  35.9 1.7 copy.7
  37.6 1.7 copy.33
  39.2 1.7 copy.32
  40.9 1.7 copy.31
  42.6 1.7 copy.30
  44.2 1.7 copy.28
  45.9 1.7 copy.27
  47.5 1.7 copy.26
  49.2 1.7 copy.25
  50.8 1.6 copy.24
  52.5 1.7 copy.23
  54.2 1.7 copy.22
  55.8 1.6 copy.21
  57.5 1.6 copy.19
  59.1 1.7 copy.18
  60.8 1.7 copy.17
  62.4 1.7 copy.16
  64.1 1.7 copy.15
  65.7 1.6 copy.14
  67.4 1.7 copy.13
  82.5 1.9 copy-done.1
  84.4 3.0 %convolution_bitcast_fusion.1 = f32[512,512]{0,1:T(8,128)} fusion(bf16[512,3456]{0,1:T(8,128)(2,1)S(1)} %constant_dynamic-update-slice_fusion, bf16[3456,512]{1,0:T(8,128)(2,1)S(1)} %bitcast.267), kind=kOutput, calls=%fused_computation.21 | convolution fusion | flops 1811939328 | bytes 8126464 | tf_op jit(solution)/shard_map/dot_general | solution.py:47
  87.5 27.6 %reduce-scatter.3.cloned.1.call-done = f32[128,512]{0,1:T(8,128)} async-done(((f32[512,512]{0,1:T(8,128)}), f32[128,512]{0,1:T(8,128)}) %reduce-scatter.3.cloned.1.call-update) | async-done | bytes 262160 | tf_op jit(solution)/shard_map/reduce_scatter | solution.py:46
  115.1 1.8 fusion.66
  116.9 5.4 %collective-permute-done.2 = bf16[1,2,16,16,128]{4,3,2,1,0:T(8,128)(2,1)} collective-permute-done((bf16[1,2,16,16,128]{4,3,2,1,0:T(8,128)(2,1)}, bf16[1,2,16,16,128]{4,3,2,1,0:T(8,128)(2,1)}, u32[]{:S(2)}, u32[]{:S(2)}) %collective-permute-start.2) | collective-permute-done | bytes 131104 | tf_op jit(solution)/shard_map/ppermute | solution.py:72
  122.3 1.9 maximum_select_fusion.3
  126.6 11.4 %collective-permute-done.3 = bf16[1,2,16,16,256]{4,3,2,1,0:T(8,128)(2,1)} collective-permute-done((bf16[1,2,16,16,256]{4,3,2,1,0:T(8,128)(2,1)}, bf16[1,2,16,16,256]{4,3,2,1,0:T(8,128)(2,1)}, u32[]{:S(2)}, u32[]{:S(2)}) %collective-permute-start.3) | collective-permute-done | bytes 262176 | tf_op jit(solution)/shard_map/ppermute | solution.py:72
  138.0 7.0 %fusion.25 = f32[27,128,512]{2,1,0:T(8,128)} fusion(bf16[27,128,512]{2,1,0:T(8,128)(2,1)} %bitcast.268, bf16[512,256]{1,0:T(8,128)(2,1)} %bitcast.56, bf16[512,256]{1,0:T(8,128)(2,1)S(1)} %maximum_select_fusion.4, pred[]{:T(512)S(6)} %eq.6), kind=kOutput, calls=%fused_computation.34 | convolution fusion | flops 1814298624 | bytes 11141121 | tf_op jit(solution)/shard_map/dot_general | solution.py:101
  147.4 3.4 %collective-permute-start.4 = (bf16[1,1,16,16,512]{4,3,2,1,0:T(8,128)(2,1)S(1)}, bf16[1,1,16,16,512]{4,3,2,1,0:T(8,128)(2,1)S(1)}, u32[]{:S(2)}, u32[]{:S(2)}) collective-permute-start(bf16[1,1,16,16,512]{4,3,2,1,0:T(8,128)(2,1)S(1)} %get-tuple-element.3), channel_id=1, source_target_pairs={{0,2},{1,3},{4,6},{5,7},{8,10},{9,11},{12,14},{13,15},{16,18},{17,... | collective-permute-start | bytes 786440 | tf_op jit(solution)/shard_map/ppermute | solution.py:17
  150.8 1.5 collective-permute-start.5
  152.2 4.2 %collective-permute-done.4 = bf16[1,1,16,16,512]{4,3,2,1,0:T(8,128)(2,1)S(1)} collective-permute-done((bf16[1,1,16,16,512]{4,3,2,1,0:T(8,128)(2,1)S(1)}, bf16[1,1,16,16,512]{4,3,2,1,0:T(8,128)(2,1)S(1)}, u32[]{:S(2)}, u32[]{:S(2)}) %collective-permute-start.4) | collective-permute-done | bytes 262176 | tf_op jit(solution)/shard_map/ppermute | solution.py:17
  156.4 4.1 %collective-permute-done.5 = bf16[1,1,16,16,512]{4,3,2,1,0:T(8,128)(2,1)S(1)} collective-permute-done((bf16[1,1,16,16,512]{4,3,2,1,0:T(8,128)(2,1)S(1)}, bf16[1,1,16,16,512]{4,3,2,1,0:T(8,128)(2,1)S(1)}, u32[]{:S(2)}, u32[]{:S(2)}) %collective-permute-start.5) | collective-permute-done | bytes 262176 | tf_op jit(solution)/shard_map/ppermute | solution.py:18
  160.6 6.7 %convolution_bitcast_fusion = f32[1,4,18,18,27,128]{5,3,4,2,1,0:T(8,128)S(1)} fusion(bf16[27,128,512]{2,1,0:T(8,128)(2,1)S(1)} %copy-done, bf16[1,1,16,16,512]{4,3,2,1,0:T(8,128)(2,1)S(1)} %collective-permute-done.5, bf16[1,2,16,16,512]{4,3,2,1,0:T(8,128)(2,1)S(1)} %maximum_select_fusion, bf16[1,1,16,16,512]{4,3,2,1,0:T(8,128)(2,1)S(1)} %collective-permute-done.4), kind=kOutput, calls=%fused_computation | convolution fusion | flops 4599078912 | bytes 22503424 | tf_op jit(solution)/shard_map/dot_general | solution.py:83
  168.5 38.5 %reduce-scatter.5.cloned.1.call-done = f32[27,128,128]{2,1,0:T(8,128)} async-done(((f32[27,128,512]{2,1,0:T(8,128)}), f32[27,128,128]{2,1,0:T(8,128)}) %reduce-scatter.5.cloned.1.call-update) | async-done | bytes 1769488 | tf_op jit(solution)/shard_map/reduce_scatter | solution.py:105
  207.0 2.9 %broadcast_multiply_fusion = f32[27,128,128]{2,1,0:T(8,128)} fusion(f32[27,128,128]{2,1,0:T(8,128)} %reduce-scatter.5.cloned.1.call-done), kind=kLoop, calls=%fused_computation.27 | loop fusion | flops 442368 | bytes 3538944 | tf_op jit(solution)/shard_map/mul | solution.py:107
  (74 shorter events, 21.2 us)
Async XLA Ops:
  7.2 75.4 %copy-start = (bf16[27,128,512]{2,1,0:T(8,128)(2,1)S(1)}, bf16[27,128,512]{2,1,0:T(8,128)(2,1)}, u32[]{:S(2)}) copy-start(bf16[27,128,512]{2,1,0:T(8,128)(2,1)} %param.5) | copy-start | bytes 10616836
  7.2 107.9 %reduce-scatter.3.cloned.1.call-start = ((), (), s32[]{:S(2)}) async-start(), calls=%async_computation.2 | async-start | bytes 1310720 | tf_op jit(solution)/shard_map/reduce_scatter | solution.py:46
  8.9 8.4 %collective-permute-start = (bf16[1,1,16,16,128]{4,3,2,1,0:T(8,128)(2,1)}, bf16[1,1,16,16,128]{4,3,2,1,0:T(8,128)(2,1)}, u32[]{:S(2)}, u32[]{:S(2)}) collective-permute-start(bf16[1,1,16,16,128]{4,3,2,1,0:T(8,128)(2,1)} %get-tuple-element.33), channel_id=1, source_target_pairs={{0,2},{1,3},{4,6},{5,7},{8,10},{9,11},{12,14},{13,15},{16,18},{17,... | collective-permute-start | bytes 196616 | tf_op jit(solution)/shard_map/ppermute | solution.py:17
  14.4 6.5 %collective-permute-start.1 = (bf16[1,1,16,16,128]{4,3,2,1,0:T(8,128)(2,1)}, bf16[1,1,16,16,128]{4,3,2,1,0:T(8,128)(2,1)}, u32[]{:S(2)}, u32[]{:S(2)}) collective-permute-start(bf16[1,1,16,16,128]{4,3,2,1,0:T(8,128)(2,1)} %get-tuple-element.34), channel_id=1, source_target_pairs={{2,0},{3,1},{6,4},{7,5},{10,8},{11,9},{14,12},{15,13},{18,16},{19,... | collective-permute-start | bytes 196616 | tf_op jit(solution)/shard_map/ppermute | solution.py:18
  17.3 7.0 %copy-start.2 = (bf16[1,2,16,16,128]{4,3,2,1,0:T(8,128)(2,1)S(1)}, bf16[1,2,16,16,128]{4,3,2,1,0:T(8,128)(2,1)}, u32[]{:S(2)}) copy-start(bf16[1,2,16,16,128]{4,3,2,1,0:T(8,128)(2,1)} %param.4) | copy-start | bytes 393220
  69.0 13.1 %copy-start.15 = (bf16[512,128]{0,1:T(8,128)(2,1)S(1)}, bf16[512,128]{0,1:T(8,128)(2,1)}, u32[]{:S(2)}) copy-start(bf16[512,128]{0,1:T(8,128)(2,1)} %copy.21) | copy-start | bytes 393220
  69.0 13.1 %copy-start.14 = (bf16[512,128]{0,1:T(8,128)(2,1)S(1)}, bf16[512,128]{0,1:T(8,128)(2,1)}, u32[]{:S(2)}) copy-start(bf16[512,128]{0,1:T(8,128)(2,1)} %copy.22) | copy-start | bytes 393220
  69.0 13.2 %copy-start.13 = (bf16[512,128]{0,1:T(8,128)(2,1)S(1)}, bf16[512,128]{0,1:T(8,128)(2,1)}, u32[]{:S(2)}) copy-start(bf16[512,128]{0,1:T(8,128)(2,1)} %copy.23) | copy-start | bytes 393220
  69.0 13.2 %copy-start.12 = (bf16[512,128]{0,1:T(8,128)(2,1)S(1)}, bf16[512,128]{0,1:T(8,128)(2,1)}, u32[]{:S(2)}) copy-start(bf16[512,128]{0,1:T(8,128)(2,1)} %copy.24) | copy-start | bytes 393220
  69.1 13.2 %copy-start.11 = (bf16[512,128]{0,1:T(8,128)(2,1)S(1)}, bf16[512,128]{0,1:T(8,128)(2,1)}, u32[]{:S(2)}) copy-start(bf16[512,128]{0,1:T(8,128)(2,1)} %copy.25) | copy-start | bytes 393220
  69.1 13.2 %copy-start.10 = (bf16[512,128]{0,1:T(8,128)(2,1)S(1)}, bf16[512,128]{0,1:T(8,128)(2,1)}, u32[]{:S(2)}) copy-start(bf16[512,128]{0,1:T(8,128)(2,1)} %copy.26) | copy-start | bytes 393220
  69.1 13.2 %copy-start.9 = (bf16[512,128]{0,1:T(8,128)(2,1)S(1)}, bf16[512,128]{0,1:T(8,128)(2,1)}, u32[]{:S(2)}) copy-start(bf16[512,128]{0,1:T(8,128)(2,1)} %copy.27) | copy-start | bytes 393220
  69.1 13.3 %copy-start.8 = (bf16[512,128]{0,1:T(8,128)(2,1)S(1)}, bf16[512,128]{0,1:T(8,128)(2,1)}, u32[]{:S(2)}) copy-start(bf16[512,128]{0,1:T(8,128)(2,1)} %copy.28) | copy-start | bytes 393220
  69.1 13.3 %copy-start.3 = (bf16[512,128]{0,1:T(8,128)(2,1)S(1)}, bf16[512,128]{0,1:T(8,128)(2,1)}, u32[]{:S(2)}) copy-start(bf16[512,128]{0,1:T(8,128)(2,1)} %copy.29) | copy-start | bytes 393220
  69.1 13.3 %copy-start.7 = (bf16[512,128]{0,1:T(8,128)(2,1)S(1)}, bf16[512,128]{0,1:T(8,128)(2,1)}, u32[]{:S(2)}) copy-start(bf16[512,128]{0,1:T(8,128)(2,1)} %copy.30) | copy-start | bytes 393220
  69.1 13.3 %copy-start.6 = (bf16[512,128]{0,1:T(8,128)(2,1)S(1)}, bf16[512,128]{0,1:T(8,128)(2,1)}, u32[]{:S(2)}) copy-start(bf16[512,128]{0,1:T(8,128)(2,1)} %copy.31) | copy-start | bytes 393220
  69.1 13.3 %copy-start.5 = (bf16[512,128]{0,1:T(8,128)(2,1)S(1)}, bf16[512,128]{0,1:T(8,128)(2,1)}, u32[]{:S(2)}) copy-start(bf16[512,128]{0,1:T(8,128)(2,1)} %copy.32) | copy-start | bytes 393220
  69.1 13.4 %copy-start.4 = (bf16[512,128]{0,1:T(8,128)(2,1)S(1)}, bf16[512,128]{0,1:T(8,128)(2,1)}, u32[]{:S(2)}) copy-start(bf16[512,128]{0,1:T(8,128)(2,1)} %copy.33) | copy-start | bytes 393220
  82.5 1.9 copy-start.1
  84.4 30.7 %copy-start.16 = (f32[128]{0:T(128)S(1)}, f32[128]{0:T(128)}, u32[]{:S(2)}) copy-start(f32[128]{0:T(128)} %param.6) | copy-start | bytes 1540
  87.5 119.5 %reduce-scatter.5.cloned.1.call-start = ((), (), s32[]{:S(2)}) async-start(), calls=%async_computation.3 | async-start | bytes 8847360 | tf_op jit(solution)/shard_map/reduce_scatter | solution.py:105
  116.9 5.4 %collective-permute-start.2 = (bf16[1,2,16,16,128]{4,3,2,1,0:T(8,128)(2,1)}, bf16[1,2,16,16,128]{4,3,2,1,0:T(8,128)(2,1)}, u32[]{:S(2)}, u32[]{:S(2)}) collective-permute-start(bf16[1,2,16,16,128]{4,3,2,1,0:T(8,128)(2,1)} %bitcast.33), channel_id=1, source_target_pairs={{0,4},{4,0},{8,12},{12,8},{1,5},{5,1},{9,13},{13,9},{2,6},{6,2},{1... | collective-permute-start | bytes 393224 | tf_op jit(solution)/shard_map/ppermute | solution.py:72
  124.2 13.8 %collective-permute-start.3 = (bf16[1,2,16,16,256]{4,3,2,1,0:T(8,128)(2,1)}, bf16[1,2,16,16,256]{4,3,2,1,0:T(8,128)(2,1)}, u32[]{:S(2)}, u32[]{:S(2)}) collective-permute-start(bf16[1,2,16,16,256]{4,3,2,1,0:T(8,128)(2,1)} %maximum_select_fusion.3), channel_id=1, source_target_pairs={{0,8},{4,12},{8,0},{12,4},{1,9},{5,13},{9,1},{13,5},{2,10},{6,14},... | collective-permute-start | bytes 786440 | tf_op jit(solution)/shard_map/ppermute | solution.py:72
  147.4 9.1 %collective-permute-start.4 = (bf16[1,1,16,16,512]{4,3,2,1,0:T(8,128)(2,1)S(1)}, bf16[1,1,16,16,512]{4,3,2,1,0:T(8,128)(2,1)S(1)}, u32[]{:S(2)}, u32[]{:S(2)}) collective-permute-start(bf16[1,1,16,16,512]{4,3,2,1,0:T(8,128)(2,1)S(1)} %get-tuple-element.3), channel_id=1, source_target_pairs={{0,2},{1,3},{4,6},{5,7},{8,10},{9,11},{12,14},{13,15},{16,18},{17,... | collective-permute-start | bytes 786440 | tf_op jit(solution)/shard_map/ppermute | solution.py:17
  150.8 9.8 %collective-permute-start.5 = (bf16[1,1,16,16,512]{4,3,2,1,0:T(8,128)(2,1)S(1)}, bf16[1,1,16,16,512]{4,3,2,1,0:T(8,128)(2,1)S(1)}, u32[]{:S(2)}, u32[]{:S(2)}) collective-permute-start(bf16[1,1,16,16,512]{4,3,2,1,0:T(8,128)(2,1)S(1)} %get-tuple-element.4), channel_id=1, source_target_pairs={{2,0},{3,1},{6,4},{7,5},{10,8},{11,9},{14,12},{15,13},{18,16},{19,... | collective-permute-start | bytes 786440 | tf_op jit(solution)/shard_map/ppermute | solution.py:18
Sparse Core Ops, SparseCore 0:
  87.6 27.4 reduce-scatter.2
  145.1 61.8 reduce-scatter.4
